TPU v7x, 32 devices: a whole 2x2x4 slice. The times are simulated.
32 devices in a mesh: group: 2 (over x), weight: 16 (over z, y, core).
Axes of the slice: x: 2, y: 2, z: 4, core: 2. Of those that a mesh axis runs over, the one named last changes fastest.
Arguments:
- hidden_in: bfloat16 [1024, 8192], P('group', 'weight'), parts along dimension 0, may hold values from -20 to 20
- norm_gain: bfloat16 [8192], P('weight'), may hold values from 0.5 to 4.5
- w_query: bfloat16 [8192, 8192], P(None, 'weight'), may hold values from -4 to 4
- w_key: bfloat16 [8192, 1024], P(None, 'weight'), may hold values from -4 to 4
- w_value: bfloat16 [8192, 1024], P(None, 'weight'), may hold values from -0.0625 to 0.0625
- w_out: bfloat16 [8192, 8192], P(None, 'weight'), may hold values from -0.0625 to 0.0625
- segment_ids: int32 [1024], P('group'), parts along dimension 0, may hold values from 0 to 31, never falling along the last dimension, each value on 1 to 32 neighbouring positions
Outputs:
- mixed: bfloat16 [1024, 8192], P('group', 'weight'), parts along dimension 0
There are 2 independent parts, one for each index of `group`. A program takes and returns all parts, laid end to end along the dimension named above; an argument that names none is the same for every part. Nothing has to cross between parts.
All inputs are finite; a program needn't handle non-finite values.
Results may differ from a plain program's by a relative error of at most 0.0065.
Values may be sent and summed in bfloat16 or wider, within the bound.
A program may use at most 128 MiB of HBM per device.

v0:
```python
import jax
import jax.numpy as jnp
from jax import lax
from jax.sharding import PartitionSpec as P

KVH = 8
HD = 128


def partner(shard, axis, bit):
    return lax.ppermute(shard, axis, [(i, i ^ 1 << bit) for i in range(lax.axis_size(axis))])


def rotate(values, position):
    half = values.shape[-1] // 2
    steps = jnp.arange(half, dtype=jnp.float32)
    freq = jnp.exp(-(2.0 * steps / (2 * half)) * jnp.log(jnp.float32(500000.0)))
    angle = position[:, None] * freq[None, :]
    cosine = jnp.cos(angle)[:, None, :]
    sine = jnp.sin(angle)[:, None, :]
    first = values[..., :half]
    second = values[..., half:]
    return jnp.concatenate(
        [first * cosine - second * sine, second * cosine + first * sine], axis=-1
    )


def add_product(piece, weights):
    return jnp.dot(piece, weights, preferred_element_type=jnp.float32)


def body(hidden_in, norm_gain, w_query, w_key, w_value, w_out, segment_ids):
    count = hidden_in.shape[0]
    as_float = hidden_in.astype(jnp.float32)
    full_rows, full_gain = (
        lax.all_gather(hidden_in, "weight", axis=1, tiled=True),
        lax.all_gather(norm_gain[None, :], "weight", axis=1, tiled=True),
    )
    rows_float = full_rows.astype(jnp.float32)
    mean_sq = jnp.mean(rows_float * rows_float, axis=1, keepdims=True)
    normed = (rows_float * lax.rsqrt(mean_sq + 1e-05) * full_gain.astype(jnp.float32)).astype(
        jnp.bfloat16
    )
    query_raw = jnp.dot(normed, w_query, preferred_element_type=jnp.float32)
    key_acc = jnp.dot(normed, w_key, preferred_element_type=jnp.float32)
    value_acc = jnp.dot(normed, w_value, preferred_element_type=jnp.float32)
    key_local = key_acc.astype(jnp.bfloat16)
    value_local = value_acc.astype(jnp.bfloat16)
    head_count = w_query.shape[1] // HD
    block_size = lax.axis_size("weight") // KVH
    my_index = lax.axis_index("weight")
    key_head, value_head = (key_local, value_local)
    for bit_number in range(block_size.bit_length() - 1):
        other_key, other_value = partner((key_head, value_head), "weight", bit_number)
        upper_half = my_index >> bit_number & 1 == 1
        key_head = jnp.where(
            upper_half,
            jnp.concatenate([other_key, key_head], axis=1),
            jnp.concatenate([key_head, other_key], axis=1),
        )
        value_head = jnp.where(
            upper_half,
            jnp.concatenate([other_value, value_head], axis=1),
            jnp.concatenate([value_head, other_value], axis=1),
        )
    index = jnp.arange(count, dtype=jnp.int32)
    same = segment_ids[:, None] == segment_ids[None, :]
    start_index = jnp.min(jnp.where(same, index[None, :], count), axis=1)
    position = (index - start_index).astype(jnp.float32)
    keep = same & (index[None, :] <= index[:, None])
    query = rotate(query_raw.reshape(count, head_count, HD), position).astype(jnp.bfloat16)
    key_rot = rotate(key_head.astype(jnp.float32).reshape(count, 1, HD), position).astype(
        jnp.bfloat16
    )[:, 0, :]
    scores = jnp.einsum(
        "thd,sd->hts", query, key_rot, preferred_element_type=jnp.float32
    ) / jnp.sqrt(jnp.float32(HD))
    scores = jnp.where(keep[None, :, :], scores, -jnp.inf)
    top = jnp.max(scores, axis=2, keepdims=True)
    probs = jnp.exp(scores - top)
    total = jnp.sum(probs, axis=2)
    weights = probs.astype(jnp.bfloat16)
    summed = jnp.einsum("hts,sd->thd", weights, value_head, preferred_element_type=jnp.float32)
    heads = (
        (summed / jnp.transpose(total)[:, :, None])
        .astype(jnp.bfloat16)
        .reshape(count, head_count * HD)
    )
    project = add_product(lax.all_gather(heads, "weight", axis=1, tiled=True), w_out)
    return (as_float + project).astype(jnp.bfloat16)


def solution(mesh):
    placed = (
        P("group", "weight"),
        P("weight"),
        P(None, "weight"),
        P(None, "weight"),
        P(None, "weight"),
        P(None, "weight"),
        P("group"),
    )
    return jax.shard_map(
        body, mesh=mesh, in_specs=placed, out_specs=P("group", "weight"), check_vma=False
    )
```

profile of v0, /device:TPU:1, one launch (start us, length us, event | category | flops | bytes accessed | tf_op | source)
XLA Modules:
  0.0 218.5 jit_solution(10447881396367661062)
XLA Ops:
  6.5 0.0 copy-start
  6.5 0.0 all-gather.5.cloned.1.call-start
  6.5 0.7 all-gather.5.cloned.1.call-update
  7.3 0.0 all-gather.7.cloned.1.call-start
  7.3 0.7 reshape.241
  8.0 23.3 %all-gather.1 = bf16[16,1,512]{2,1,0:T(2,128)(2,1)S(1)} all-gather(bf16[1,1,512]{2,1,0:T(2,128)(2,1)S(1)} %reshape.241), channel_id=2, replica_groups=mesh['group'=2,'weight'=16] {'weight'}, dimensions={0}, use_global_device_ids=true | all-gather | bytes 17408 | tf_op jit(solution)/shard_map/all_gather | solution.py:37
  31.3 1.0 fusion.13
  32.3 1.0 compare_and_fusion
  33.3 1.8 multiply_cosine_fusion
  35.1 55.1 %all-gather.5.cloned.1.call-done = bf16[512,8192]{1,0:T(8,128)(2,1)} async-done(((bf16[512,512]{1,0:T(8,128)(2,1)}), bf16[512,8192]{1,0:T(8,128)(2,1)}) %all-gather.5.cloned.1.call-update) | async-done | bytes 8388624 | tf_op jit(solution)/shard_map/all_gather | solution.py:36
  90.2 5.1 %fusion = f32[512]{0:T(512)S(1)} fusion(bf16[512,8192]{1,0:T(8,128)(2,1)} %all-gather.5.cloned.1.call-done), kind=kLoop, calls=%fused_computation.2 | loop fusion | flops 12582400 | bytes 8390656 | tf_op jit(solution)/shard_map/reduce_sum | solution.py:40
  95.3 11.5 %fusion.45 = f32[512,512]{0,1:T(8,128)S(1)} fusion(bf16[8192,512]{1,0:T(8,128)(2,1)} %param.9, bf16[512,8192]{1,0:T(8,128)(2,1)} %all-gather.5.cloned.1.call-done, f32[8192]{0:T(1024)S(1)} %bitcast.46, f32[512]{0:T(512)S(1)} %add_rsqrt_fusion), kind=kOutput, calls=%fused_computation.62 | convolution fusion | flops 4311744512 | bytes 17860608 | tf_op jit(solution)/shard_map/dot_general | solution.py:44
  106.8 0.0 slice-start
  106.9 0.9 fusion.49
  107.7 0.0 copy-done
  107.7 0.0 slice-start.1
  107.7 0.0 copy-start.2
  107.7 7.3 %convolution_convert_fusion.1 = bf16[512,64]{0,1:T(8,128)(2,1)} fusion(bf16[8192,64]{0,1:T(8,128)(2,1)S(1)} %copy-done, bf16[512,8192]{1,0:T(8,128)(2,1)} %all-gather.5.cloned.1.call-done, f32[8192]{0:T(1024)S(1)} %bitcast.47, f32[512]{0:T(512)S(1)} %add_rsqrt_fusion), kind=kOutput, calls=%fused_computation.18 | convolution fusion | flops 553680896 | bytes 9537536 | tf_op jit(solution)/shard_map/dot_general | solution.py:46
  115.0 0.3 collective-permute-start
  115.3 0.0 slice-done
  115.3 0.0 slice-done.1
  115.3 0.0 copy-done.2
  115.3 2.9 %convolution_convert_fusion = bf16[512,64]{0,1:T(8,128)(2,1)S(1)} fusion(bf16[8192,64]{0,1:T(8,128)(2,1)S(1)} %copy-done.2, bf16[512,8192]{1,0:T(8,128)(2,1)S(1)} %bitcast.41, f32[8192]{0:T(1024)S(1)} %bitcast.48, f32[512]{0:T(512)S(1)} %add_rsqrt_fusion), kind=kOutput, calls=%fused_computation.17 | convolution fusion | flops 553680896 | bytes 9537536 | tf_op jit(solution)/shard_map/dot_general | solution.py:45
  118.2 0.3 collective-permute-start.1
  118.5 0.3 copy.20
  118.8 1.4 copy.19
  120.2 1.3 subtract_convert_fusion
  121.5 0.0 collective-permute-done.1
  121.6 0.6 fusion.40
  122.1 1.2 fusion.5
  123.3 0.0 copy-start.1
  123.3 0.9 fusion.3
  124.3 0.0 collective-permute-done
  124.3 3.1 %divide_convert_fusion = bf16[512,4,128]{0,2,1:T(8,128)(2,1)} fusion(f32[512,512,4]{1,0,2:T(8,128)S(1)} %get-tuple-element.14, f32[4,512]{1,0:T(4,128)S(1)} %get-tuple-element.13, pred[512,512]{0,1:T(8,128)(4,1)S(1)} %compare_and_fusion, f32[512,4]{0,1:T(4,128)S(1)} %bitcast.49, bf16[512,64]{0,1:T(8,128)(2,1)} %convolution_convert_fusion.1, ...), kind=kOutput, calls=%fused_computation.20 | convolution fusion | flops 273743872 | bytes 5128193 | tf_op jit(solution)/shard_map/hts,sd->thd/dot_general | solution.py:83
  127.4 0.0 all-gather.7.cloned.1.call-update
  127.4 73.2 %all-gather.7.cloned.1.call-done = bf16[512,8192]{0,1:T(8,128)(2,1)} async-done(((bf16[512,512]{0,1:T(8,128)(2,1)}), bf16[512,8192]{0,1:T(8,128)(2,1)}) %all-gather.7.cloned.1.call-update) | async-done | bytes 8388624 | tf_op jit(solution)/shard_map/all_gather | solution.py:89
  200.6 0.0 copy-done.1
  200.6 11.1 %fusion.12 = bf16[512,512]{1,0:T(8,128)(2,1)} fusion(bf16[512,8192]{0,1:T(8,128)(2,1)} %all-gather.7.cloned.1.call-done, bf16[8192,512]{1,0:T(8,128)(2,1)} %param.12, bf16[512,512]{1,0:T(8,128)(2,1)S(1)} %copy-done.1), kind=kOutput, calls=%fused_computation.16 | convolution fusion | flops 4295753728 | bytes 17825792 | tf_op jit(solution)/shard_map/dot_general | solution.py:29
  (6 shorter events, 0.1 us)
Async XLA Ops:
  6.5 101.2 %copy-start = (bf16[8192,64]{0,1:T(8,128)(2,1)S(1)}, bf16[8192,64]{0,1:T(8,128)(2,1)}, u32[]{:S(2)}) copy-start(bf16[8192,64]{0,1:T(8,128)(2,1)} %param.11) | copy-start | bytes 3145732
  6.5 83.7 %all-gather.5.cloned.1.call-start = ((), (), s32[]{:S(2)}) async-start(), calls=%async_computation | async-start | bytes 8912896 | tf_op jit(solution)/shard_map/all_gather | solution.py:36
  7.3 193.4 %all-gather.7.cloned.1.call-start = ((), (), s32[]{:S(2)}) async-start(), calls=%async_computation.1 | async-start | bytes 8912896 | tf_op jit(solution)/shard_map/all_gather | solution.py:89
  106.8 8.4 %slice-start = ((s8[8388608]{0:T(1024)(128)(4,1)}), s8[4194304]{0:T(1024)(128)(4,1)S(1)}, s32[]{:S(2)}) async-start(s8[8388608]{0:T(1024)(128)(4,1)} %bitcast.40), calls=%async_computation.2 | async-start | bytes 8388608
  107.7 7.5 %slice-start.1 = ((s8[8388608]{0:T(1024)(128)(4,1)}), s8[4194304]{0:T(1024)(128)(4,1)S(1)}, s32[]{:S(2)}) async-start(s8[8388608]{0:T(1024)(128)(4,1)} %bitcast.40), calls=%async_computation.3 | async-start | bytes 8388608
  107.7 7.5 %copy-start.2 = (bf16[8192,64]{0,1:T(8,128)(2,1)S(1)}, bf16[8192,64]{0,1:T(8,128)(2,1)}, u32[]{:S(2)}) copy-start(bf16[8192,64]{0,1:T(8,128)(2,1)} %param.10) | copy-start | bytes 3145732
  115.0 9.2 %collective-permute-start = (bf16[512,64]{0,1:T(8,128)(2,1)}, bf16[512,64]{0,1:T(8,128)(2,1)}, u32[]{:S(2)}, u32[]{:S(2)}) collective-permute-start(bf16[512,64]{0,1:T(8,128)(2,1)} %convolution_convert_fusion.1), channel_id=1, source_target_pairs={{0,1},{1,0},{2,3},{3,2},{4,5},{5,4},{6,7},{7,6},{8,9},{9,8},{10,11... | collective-permute-start | bytes 196616 | tf_op jit(solution)/shard_map/ppermute | solution.py:11
  118.2 3.4 %collective-permute-start.1 = (bf16[512,64]{0,1:T(8,128)(2,1)S(1)}, bf16[512,64]{0,1:T(8,128)(2,1)S(1)}, u32[]{:S(2)}, u32[]{:S(2)}) collective-permute-start(bf16[512,64]{0,1:T(8,128)(2,1)S(1)} %convolution_convert_fusion), channel_id=1, source_target_pairs={{0,1},{1,0},{2,3},{3,2},{4,5},{5,4},{6,7},{7,6},{8,9},{9,8},{10,11... | collective-permute-start | bytes 196616 | tf_op jit(solution)/shard_map/ppermute | solution.py:11
  123.3 77.3 %copy-start.1 = (bf16[512,512]{1,0:T(8,128)(2,1)S(1)}, bf16[512,512]{1,0:T(8,128)(2,1)}, u32[]{:S(2)}) copy-start(bf16[512,512]{1,0:T(8,128)(2,1)} %param.7) | copy-start | bytes 1572868
Sparse Core Ops, SparseCore 0:
  9.5 80.6 all-gather.4
  127.5 73.0 all-gather.6
where the time goes:
time: 219 us
  waiting for transfers between devices  129 us (59%)
  matrix products  37 us (17%)
  blocking collectives  23.3 us (11%)
  between operations  13.5 us (6%)
  other arithmetic  11.7 us (5%)
  local copies, waits for them, and re-layouts  3.29 us (2%)
    all_gather x1, waiting for transfers between devices, body(): lax.all_gather(heads, 'weight', axis=1, tiled=True)  73.2 us
    all_gather x1, waiting for transfers between devices, body(): lax.all_gather(hidden_in, 'weight', axis=1, tiled=True)  55.1 us
    all_gather x1, blocking collectives, body(): lax.all_gather(norm_gain[None, :], 'weight', axis=1, tiled=True)  23.3 us
    dot_general x1, matrix products, body(): query_raw = jnp.dot(normed, w_query, preferred_element_type=jnp.float32)  11.5 us
    dot_general x1, matrix products, add_product(): return jnp.dot(piece, weights, preferred_element_type=jnp.float32)  11.1 us
    dot_general x1, matrix products, body(): value_acc = jnp.dot(normed, w_value, preferred_element_type=jnp.float32)  7.29 us
    reduce_sum x1, other arithmetic, body(): mean_sq = jnp.mean(rows_float * rows_float, axis=1, keepdims=True)  5.1 us
  transfers between devices with their start and end apart: 4, of which 2 were waited for; matrix products, arithmetic and copies ran while one was open for 6% of the time, Pallas kernels for 0%

commit v1 on v0

--- a/solution.py
+++ b/solution.py
@@ -1,6 +1,10 @@
+import functools
+
 import jax
 import jax.numpy as jnp
 from jax import lax
+from jax.experimental import pallas as pl
+from jax.experimental.pallas import tpu as pltpu
 from jax.sharding import PartitionSpec as P
 
 KVH = 8
@@ -90,6 +94,364 @@
     return (as_float + project).astype(jnp.bfloat16)
 
 
+def dot(a, b):
+    return jnp.dot(a, b, preferred_element_type=jnp.float32)
+
+
+def spread(row, height):
+    return jnp.broadcast_to(row, (height, row.shape[1])).T
+
+
+def fused(
+    n, hidden, gain, w_query, w_key, w_value, w_out, seg, out,
+    buf, vq, vk, vv, vo, acc_q, acc_k, acc_v, acc_o, stats, rcol, cos_tab, sin_tab, bias,
+    kv, kbuf, vbuf, load_sem, ring_send, ring_recv, sib_send, sib_recv,
+    stat_send, stat_recv, kv_send, kv_recv,
+):
+    f32, bf16 = jnp.float32, jnp.bfloat16
+    tokens, width = hidden.shape
+    rows = tokens // 2
+    piece = rows // 2
+    heads = width // HD
+    half = HD // 2
+    chips = n // 2
+    zs = chips // 2
+    me = lax.axis_index("weight")
+    core = me % 2
+    chip = me // 2
+    pos = (chip // 2) * (1 - chip % 2) + (2 * zs - 1 - chip // 2) * (chip % 2)
+    sib = me + 1 - 2 * core
+
+    def chip_at(place):
+        place = (place + 2 * chips) % chips
+        y = place // zs
+        z = place * (1 - y) + (2 * zs - 1 - place) * y
+        return z * 2 + y
+
+    def at(place):
+        return chip_at(place) * 2 + core
+
+    peers = (at(pos + 1), at(pos - 1))
+
+    def remote(src, dst, send, recv, target):
+        return pltpu.make_async_remote_copy(
+            src_ref=src, dst_ref=dst, send_sem=send, recv_sem=recv,
+            device_id={"weight": target}, device_id_type=pl.DeviceIdType.MESH,
+        )
+
+    def ring(way, stage, step, part):
+        owner = at(pos - step) if way == 0 else at(pos + step)
+        ref = buf.at[stage, owner, pl.ds(part * piece, piece)]
+        return remote(
+            ref, ref, ring_send.at[way, stage, step, part], ring_recv.at[way, stage, step, part],
+            peers[way],
+        )
+
+    def arrival(way, stage, step, part):
+        owner = at(pos - step - 1) if way == 0 else at(pos + step + 1)
+        ref = buf.at[stage, owner, pl.ds(part * piece, piece)]
+        return remote(
+            ref, ref, ring_send.at[way, stage, step, part], ring_recv.at[way, stage, step, part],
+            peers[way],
+        )
+
+    def share(stage, slot, place, own):
+        owner = chip_at(place) * 2 + (core if own else 1 - core)
+        ref = buf.at[stage, owner]
+        return remote(ref, ref, sib_send.at[stage, slot], sib_recv.at[stage, slot], sib)
+
+    def send_own(stage):
+        for part in range(2):
+            for way in range(2):
+                ring(way, stage, 0, part).start()
+        share(stage, 0, pos, True).start()
+
+    def kv_copy(stage, side):
+        ref = kv.at[stage, side]
+        return remote(ref, ref, kv_send.at[stage], kv_recv.at[stage], sib)
+
+    own_x = [
+        pltpu.make_async_copy(
+            hidden.at[pl.ds(stage * rows, rows)], buf.at[stage, me], load_sem.at[4 + stage]
+        )
+        for stage in range(2)
+    ]
+    for copy in own_x:
+        copy.start()
+    loads = [
+        pltpu.make_async_copy(src, dst, load_sem.at[i])
+        for i, (src, dst) in enumerate(
+            ((w_query, vq), (w_key, vk), (w_value, vv), (w_out, vo))
+        )
+    ]
+    for copy in loads:
+        copy.start()
+
+    barrier = pltpu.get_barrier_semaphore()
+
+    def greet(i, carry):
+        pl.semaphore_signal(
+            barrier, inc=1, device_id={"weight": (me + i) % n},
+            device_id_type=pl.DeviceIdType.MESH,
+        )
+        return carry
+
+    lax.fori_loop(1, n, greet, 0)
+    for copy in own_x:
+        copy.wait()
+    pl.semaphore_wait(barrier, n - 1)
+    send_own(0)
+
+    squares = []
+    for stage in range(2):
+        values = buf[stage, me].astype(f32)
+        squares.append(jnp.sum(values * values, axis=1, keepdims=True))
+    column = jnp.broadcast_to(jnp.concatenate(squares, axis=0), (tokens, 128))
+    upper = lax.broadcasted_iota(jnp.int32, (8, width), 0) < 4
+    own_gain = jnp.broadcast_to(gain[...].astype(f32), (8, width))
+    stats[me] = jnp.where(upper, column.T[0:8], own_gain)
+
+    def stat_copy(i, owner):
+        ref = stats.at[owner]
+        return remote(ref, ref, stat_send.at[i], stat_recv.at[i], (me + i) % n)
+
+    def send_stat(i, carry):
+        stat_copy(i, me).start()
+        return carry
+
+    lax.fori_loop(1, n, send_stat, 0)
+
+    seg_row = seg[...].astype(f32)
+    padded = jnp.concatenate([jnp.full((1, 128), -1.0, f32), seg_row], axis=1)
+    seg_col = spread(seg_row, 128)
+    window = rows + 128
+    lane = lax.broadcasted_iota(jnp.int32, (rows, HD), 1)
+    freq = jnp.exp(
+        -(2.0 * (lane % half).astype(f32) / HD) * jnp.log(jnp.float32(500000.0))
+    )
+    for stage in range(2):
+        first = stage * rows
+        col = seg_col[first:first + rows]
+        same = jnp.concatenate([col] * (window // 128), axis=1) == padded[:, first:first + window]
+        key_at = lax.broadcasted_iota(jnp.int32, (rows, window), 1) + (first - 128)
+        query_at = lax.broadcasted_iota(jnp.int32, (rows, window), 0) + first
+        bias[stage] = jnp.where(same & (key_at <= query_at), 0.0, -jnp.inf)
+        start = jnp.min(
+            jnp.where(same, key_at.astype(f32), jnp.float32(tokens)), axis=1, keepdims=True
+        )
+        token = (lax.broadcasted_iota(jnp.int32, (rows, HD), 0) + first).astype(f32)
+        angle = (token - start) * freq
+        cos_tab[stage] = jnp.cos(angle)
+        sine = jnp.sin(angle)
+        sin_tab[stage] = jnp.where(lane < half, -sine, sine)
+    acc_q[...] = jnp.zeros_like(acc_q)
+    acc_k[...] = jnp.zeros_like(acc_k)
+    acc_v[...] = jnp.zeros_like(acc_v)
+    acc_o[...] = jnp.zeros_like(acc_o)
+    kbuf[0:128] = jnp.zeros((128, HD), bf16)
+    vbuf[0:128] = jnp.zeros((128, HD), bf16)
+
+    def wait_stat(i, carry):
+        stat_copy(i, (me - i + n) % n).wait_recv()
+        return carry
+
+    lax.fori_loop(1, n, wait_stat, 0)
+    total = jnp.sum(stats[...], axis=0)[0:1]
+    scale = lax.rsqrt(total / jnp.float32(n * width) + 1e-05)
+    rcol[...] = spread(scale, 128)
+    for copy in loads:
+        copy.wait()
+
+    def turn(values, stage):
+        other = jnp.concatenate([values[:, half:], values[:, :half]], axis=1)
+        return (values * cos_tab[stage] + other * sin_tab[stage]).astype(bf16)
+
+    def project(stage, owner):
+        scale_rows = rcol[pl.ds(pl.multiple_of(stage * rows, rows), rows)]
+        wide = jnp.concatenate([scale_rows] * (width // 128), axis=1)
+        block = (
+            buf[stage, owner].astype(f32) * wide * stats[owner, 4:5]
+        ).astype(bf16)
+        depth = pl.ds(pl.multiple_of(owner * width, width), width)
+        acc_q[stage] += dot(block, vq[depth])
+        acc_k[stage] += dot(block, vk[depth])
+        acc_v[stage] += dot(block, vv[depth])
+
+    def combine(stage, owner):
+        depth = pl.ds(pl.multiple_of(owner * width, width), width)
+        acc_o[stage - 2] += dot(buf[stage, owner], vo[depth])
+
+    def use(stage, owner):
+        @pl.when(stage < 2)
+        def _():
+            project(stage, owner)
+
+        @pl.when(stage >= 2)
+        def _():
+            combine(stage, owner)
+
+    def attend(stage):
+        kv_copy(stage, 1 - core).wait_recv()
+        low, high = kv[stage, 0], kv[stage, 1]
+        keys = jnp.concatenate([low[:, :half], high[:, :half]], axis=1)
+        values = jnp.concatenate([low[:, half:], high[:, half:]], axis=1)
+        here = pl.ds(pl.multiple_of(stage * rows + 128, 128), rows)
+        kbuf[here] = turn(keys.astype(f32), stage)
+        vbuf[here] = values
+        near = pl.ds(pl.multiple_of(stage * rows, 128), window)
+        key_win = kbuf[near]
+        value_win = vbuf[near]
+        for head in range(heads):
+            cols = slice(head * HD, head * HD + HD)
+            query = turn(acc_q[stage, :, cols], stage)
+            scores = lax.dot_general(
+                query, key_win, (((1,), (1,)), ((), ())), preferred_element_type=f32
+            ) / jnp.sqrt(jnp.float32(HD)) + bias[stage]
+            probs = jnp.exp(scores - jnp.max(scores, axis=1, keepdims=True))
+            mass = jnp.sum(probs, axis=1, keepdims=True)
+            buf[stage + 2, me, :, cols] = (dot(probs.astype(bf16), value_win) / mass).astype(bf16)
+
+    def step_body(t, carry):
+        stage = t // 4
+        step = t % 4
+
+        @pl.when((step == 3) & (stage < 3))
+        def _():
+            send_own(stage + 1)
+
+        for part in range(2):
+            for way in range(2):
+                @pl.when((step < 3) | (part == way))
+                def _():
+                    arrival(way, stage, step, part).wait_recv()
+
+                @pl.when((step < 2) | ((step == 2) & (part == way)))
+                def _():
+                    ring(way, stage, step + 1, part).start()
+
+        @pl.when(step < 3)
+        def _():
+            share(stage, step + 1, pos - step - 1, True).start()
+            share(stage, step + 4, pos + step + 1, True).start()
+
+        @pl.when(step == 3)
+        def _():
+            share(stage, 7, pos + 4, True).start()
+
+        @pl.when((step == 0) & ((stage == 1) | (stage == 2)))
+        def _():
+            attend(stage - 1)
+
+        def unit(u, carry):
+            last = u // 2
+            left = u % 2
+            right = 1 - left - last
+            place = pos - step * right + step * left + 4 * last
+            slot = step * right + (step + 3) * left + 7 * last
+
+            @pl.when((u == 0) | ((u == 1) & (step > 0)) | ((u == 2) & (step == 3)))
+            def _():
+                share(stage, slot, place, False).wait_recv()
+                first = chip_at(place) * 2
+
+                def one(k, carry):
+                    use(stage, first + k)
+                    return carry
+
+                lax.fori_loop(0, 2, one, 0)
+
+            return carry
+
+        lax.fori_loop(0, 3, unit, 0)
+
+        @pl.when((step == 3) & (stage < 2))
+        def _():
+            kv[stage, core] = jnp.concatenate(
+                [acc_k[stage].astype(bf16), acc_v[stage].astype(bf16)], axis=1
+            )
+            kv_copy(stage, core).start()
+
+        return carry
+
+    lax.fori_loop(0, 16, step_body, 0)
+
+    for stage in range(2):
+        out[stage * rows:(stage + 1) * rows] = (
+            buf[stage, me].astype(f32) + acc_o[stage]
+        ).astype(bf16)
+
+    def finish(stage, carry):
+        for way in range(2):
+            for step in range(4):
+                for part in range(2):
+                    if step < 3 or part == way:
+                        ring(way, stage, step, part).wait_send()
+        for slot, away in enumerate((0, -1, -2, -3, 1, 2, 3, 4)):
+            share(stage, slot, pos + away, True).wait_send()
+        return carry
+
+    lax.fori_loop(0, 4, finish, 0)
+    for stage in range(2):
+        kv_copy(stage, core).wait_send()
+
+    def left(i, carry):
+        stat_copy(i, me).wait_send()
+        return carry
+
+    lax.fori_loop(1, n, left, 0)
+
+
+def ring_body(hidden_in, norm_gain, w_query, w_key, w_value, w_out, segment_ids):
+    n = lax.axis_size("weight")
+    tokens, width = hidden_in.shape
+    depth = w_query.shape[0]
+    rows = tokens // 2
+    kvw = w_key.shape[1]
+    f32, bf16 = jnp.float32, jnp.bfloat16
+    anywhere = pl.BlockSpec(memory_space=pl.ANY)
+    vmem = pl.BlockSpec(memory_space=pltpu.VMEM)
+    dma = pltpu.SemaphoreType.DMA
+    return pl.pallas_call(
+        functools.partial(fused, n),
+        out_shape=jax.ShapeDtypeStruct((tokens, width), bf16),
+        in_specs=[anywhere, vmem, anywhere, anywhere, anywhere, anywhere, vmem],
+        out_specs=vmem,
+        scratch_shapes=[
+            pltpu.VMEM((4, n, rows, width), bf16),
+            pltpu.VMEM(w_query.shape, bf16),
+            pltpu.VMEM(w_key.shape, bf16),
+            pltpu.VMEM(w_value.shape, bf16),
+            pltpu.VMEM(w_out.shape, bf16),
+            pltpu.VMEM((2, rows, w_query.shape[1]), f32),
+            pltpu.VMEM((2, rows, kvw), f32),
+            pltpu.VMEM((2, rows, kvw), f32),
+            pltpu.VMEM((2, rows, width), f32),
+            pltpu.VMEM((n, 8, tokens), f32),
+            pltpu.VMEM((tokens, 128), f32),
+            pltpu.VMEM((2, rows, HD), f32),
+            pltpu.VMEM((2, rows, HD), f32),
+            pltpu.VMEM((2, rows, rows + 128), f32),
+            pltpu.VMEM((2, 2, rows, 2 * kvw), bf16),
+            pltpu.VMEM((tokens + 128, HD), bf16),
+            pltpu.VMEM((tokens + 128, HD), bf16),
+            dma((6,)),
+            dma((2, 4, 4, 2)),
+            dma((2, 4, 4, 2)),
+            dma((4, 8)),
+            dma((4, 8)),
+            dma((n,)),
+            dma((n,)),
+            dma((2,)),
+            dma((2,)),
+        ],
+        compiler_params=pltpu.CompilerParams(
+            collective_id=0, has_side_effects=True, vmem_limit_bytes=56 * 1024 * 1024
+        ),
+    )(
+        hidden_in, norm_gain[None, :], w_query, w_key, w_value, w_out, segment_ids[None, :]
+    )
+
+
 def solution(mesh):
     placed = (
         P("group", "weight"),
@@ -100,6 +462,7 @@
         P(None, "weight"),
         P("group"),
     )
+    chosen = ring_body if mesh.shape["weight"] == 2 * KVH else body
     return jax.shard_map(
-        body, mesh=mesh, in_specs=placed, out_specs=P("group", "weight"), check_vma=False
-    )
+        chosen, mesh=mesh, in_specs=placed, out_specs=P("group", "weight"), check_vma=False
+    )

time: 219 us -> 117 us (0.53)
  waiting for transfers between devices: 129 us -> 0 us
  Pallas kernels: 0 us -> 108 us
  matrix products: 37 us -> 0 us
  blocking collectives: 23.3 us -> 0 us
  between operations: 13.5 us -> 0.01 us
  other arithmetic: 11.7 us -> 0 us
  local copies, waits for them, and re-layouts: 3.29 us -> 8.63 us
    all_gather x2 -> x0, waiting for transfers between devices: 128 us -> none  [the longest x1 73.2 us: body(): lax.all_gather(heads, 'weight', axis=1, tiled=True)]
    pallas_call x0 -> x1, Pallas kernels: none -> 108 us  [ring_body(): pl.pallas_call(functools.partial(fused, n), out_shape=jax.ShapeDtypeStruc...]
    dot_general x6 -> x0, matrix products: 37 us -> none  [the longest x1 11.5 us: body(): query_raw = jnp.dot(normed, w_query, preferred_element_type=jnp.float32)]
    all_gather x1 -> x0, blocking collectives: 23.3 us -> none  [body(): lax.all_gather(norm_gain[None, :], 'weight', axis=1, tiled=True)]
    reduce_sum x2 -> x0, other arithmetic: 6.02 us -> none  [the longest x1 5.1 us: body(): mean_sq = jnp.mean(rows_float * rows_float, axis=1, keepdims=True)]
    unnamed x13 -> x3, local copies, waits for them, and re-layouts: 2.41 us -> 7.37 us
  transfers between devices with their start and end apart: 4 -> 0, of which waited for: 2 -> 0; matrix products, arithmetic and copies ran while one was open for 6% -> 0% of each run, Pallas kernels for 0% -> 0%
where the time goes in v1:
time: 117 us
  Pallas kernels  108 us (92%)
  local copies, waits for them, and re-layouts  8.63 us (7%)
    pallas_call x1, Pallas kernels, ring_body(): pl.pallas_call(functools.partial(fused, n), out_shape=jax.ShapeDtypeStruc...  108 us
    unnamed x3, local copies, waits for them, and re-layouts  7.37 us

profile of v1, /device:TPU:1, one launch (start us, length us, event | category | flops | bytes accessed | tf_op | source)
XLA Modules:
  0.0 116.5 jit_solution(17239262072302486009)
XLA Ops:
  0.0 1.3 %broadcast_in_dim.6.gain = bf16[1,512]{1,0:T(2,128)(2,1)} reshape(bf16[512]{0:T(512)(128)(2,1)} %param.8) | data formatting | bytes 2048 | tf_op jit(solution)/shard_map/broadcast_in_dim | solution.py:451
  1.3 2.8 %copy.8.w_key = bf16[8192,64]{1,0:T(8,128)(2,1)} copy(bf16[8192,64]{0,1:T(8,128)(2,1)} %param.10) | data formatting | bytes 2097152 | tf_op args[3]
  4.0 2.7 %copy.9.w_value = bf16[8192,64]{1,0:T(8,128)(2,1)} copy(bf16[8192,64]{0,1:T(8,128)(2,1)} %param.11) | data formatting | bytes 2097152 | tf_op args[4]
  6.8 107.9 %shard_map.73 = bf16[512,512]{1,0:T(8,128)(2,1)} custom-call(bf16[512,512]{1,0:T(8,128)(2,1)} %hidden.1, bf16[1,512]{1,0:T(2,128)(2,1)} %broadcast_in_dim.6.gain, bf16[8192,512]{1,0:T(8,128)(2,1)} %w_query.1, bf16[8192,64]{1,0:T(8,128)(2,1)} %copy.8.w_key, bf16[8192,64]{1,0:T(8,128)(2,1)} %copy.9.w_value, bf16[8192,512]{1,0:T(8,128)(2,1)} %w_out.1, ...), custom_call_target="tpu_custom_call" | custom-call | tf_op jit(solution)/shard_map/pallas_call | solution.py:414
  114.6 1.9 %copy.11 = bf16[512,512]{1,0:T(8,128)(2,1)} copy(bf16[512,512]{1,0:T(8,128)(2,1)} %shard_map.73) | data formatting | bytes 1048576

commit v2 on v1

--- a/solution.py
+++ b/solution.py
@@ -8,6 +8,7 @@
 from jax.sharding import PartitionSpec as P
 
 KVH = 8
+PARTS = 4
 HD = 128
 
 
@@ -98,22 +99,30 @@
     return jnp.dot(a, b, preferred_element_type=jnp.float32)
 
 
+def dot_t(a, b):
+    return lax.dot_general(
+        a, b, (((1,), (1,)), ((), ())), preferred_element_type=jnp.float32
+    )
+
+
 def spread(row, height):
     return jnp.broadcast_to(row, (height, row.shape[1])).T
 
 
 def fused(
     n, hidden, gain, w_query, w_key, w_value, w_out, seg, out,
-    buf, vq, vk, vv, vo, acc_q, acc_k, acc_v, acc_o, stats, rcol, cos_tab, sin_tab, bias,
+    buf, vq, vkv, vo, acc_q, acc_kv, acc_o, stats, rcol, seg_row, seg_col, cos_tab, sin_tab, bias,
     kv, kbuf, vbuf, load_sem, ring_send, ring_recv, sib_send, sib_recv,
     stat_send, stat_recv, kv_send, kv_recv,
 ):
     f32, bf16 = jnp.float32, jnp.bfloat16
     tokens, width = hidden.shape
     rows = tokens // 2
-    piece = rows // 2
+    piece = rows // PARTS
     heads = width // HD
     half = HD // 2
+    kvw = w_key.shape[0]
+    window = rows + 128
     chips = n // 2
     zs = chips // 2
     me = lax.axis_index("weight")
@@ -161,7 +170,7 @@
         return remote(ref, ref, sib_send.at[stage, slot], sib_recv.at[stage, slot], sib)
 
     def send_own(stage):
-        for part in range(2):
+        for part in range(PARTS):
             for way in range(2):
                 ring(way, stage, 0, part).start()
         share(stage, 0, pos, True).start()
@@ -181,7 +190,12 @@
     loads = [
         pltpu.make_async_copy(src, dst, load_sem.at[i])
         for i, (src, dst) in enumerate(
-            ((w_query, vq), (w_key, vk), (w_value, vv), (w_out, vo))
+            (
+                (w_query, vq),
+                (w_key, vkv.at[pl.ds(0, kvw)]),
+                (w_value, vkv.at[pl.ds(kvw, kvw)]),
+                (w_out, vo),
+            )
         )
     ]
     for copy in loads:
@@ -191,48 +205,79 @@
 
     def greet(i, carry):
         pl.semaphore_signal(
-            barrier, inc=1, device_id={"weight": (me + i) % n},
+            barrier, inc=1, device_id={"weight": (me + 2 * i) % n},
             device_id_type=pl.DeviceIdType.MESH,
         )
         return carry
 
-    lax.fori_loop(1, n, greet, 0)
+    lax.fori_loop(1, chips, greet, 0)
+    pl.semaphore_signal(
+        barrier, inc=1, device_id={"weight": sib}, device_id_type=pl.DeviceIdType.MESH
+    )
+    acc_q[...] = jnp.zeros_like(acc_q)
+    acc_kv[...] = jnp.zeros_like(acc_kv)
+    acc_o[...] = jnp.zeros_like(acc_o)
+    kbuf[0:128] = jnp.zeros((128, HD), bf16)
+    vbuf[0:128] = jnp.zeros((128, HD), bf16)
+    ids = seg[...].astype(f32)
+    seg_row[...] = jnp.broadcast_to(
+        jnp.concatenate([jnp.full((1, 128), -1.0, f32), ids], axis=1), seg_row.shape
+    )
+    seg_col[...] = spread(ids, 128)
     for copy in own_x:
         copy.wait()
-    pl.semaphore_wait(barrier, n - 1)
-    send_own(0)
-
-    squares = []
+
+    groups = tokens // 128
+    lines = []
     for stage in range(2):
         values = buf[stage, me].astype(f32)
-        squares.append(jnp.sum(values * values, axis=1, keepdims=True))
-    column = jnp.broadcast_to(jnp.concatenate(squares, axis=0), (tokens, 128))
-    upper = lax.broadcasted_iota(jnp.int32, (8, width), 0) < 4
-    own_gain = jnp.broadcast_to(gain[...].astype(f32), (8, width))
-    stats[me] = jnp.where(upper, column.T[0:8], own_gain)
+        sums = jnp.sum(values * values, axis=1, keepdims=True)
+        across = jnp.broadcast_to(sums, (rows, 128)).T[0:1]
+        lines += [across[:, i * 128:(i + 1) * 128] for i in range(rows // 128)]
+    own_gain = gain[...].astype(f32).reshape(1, width)
+    lines += [own_gain[:, i * 128:(i + 1) * 128] for i in range(width // 128)]
+    stats[core, chip] = jnp.concatenate(lines, axis=0)
 
     def stat_copy(i, owner):
-        ref = stats.at[owner]
-        return remote(ref, ref, stat_send.at[i], stat_recv.at[i], (me + i) % n)
+        ref = stats.at[core, owner]
+        return remote(ref, ref, stat_send.at[i], stat_recv.at[i], (me + 2 * i) % n)
+
+    def stat_share(side):
+        ref = stats.at[side]
+        return remote(ref, ref, stat_send.at[0], stat_recv.at[0], sib)
 
     def send_stat(i, carry):
-        stat_copy(i, me).start()
+        stat_copy(i, chip).start()
         return carry
 
-    lax.fori_loop(1, n, send_stat, 0)
-
-    seg_row = seg[...].astype(f32)
-    padded = jnp.concatenate([jnp.full((1, 128), -1.0, f32), seg_row], axis=1)
-    seg_col = spread(seg_row, 128)
-    window = rows + 128
-    lane = lax.broadcasted_iota(jnp.int32, (rows, HD), 1)
-    freq = jnp.exp(
-        -(2.0 * (lane % half).astype(f32) / HD) * jnp.log(jnp.float32(500000.0))
-    )
-    for stage in range(2):
+    pl.semaphore_wait(barrier, chips)
+    lax.fori_loop(1, chips, send_stat, 0)
+    send_own(0)
+
+    def prepare():
+        def wait_stat(i, carry):
+            stat_copy(i, (chip - i + chips) % chips).wait_recv()
+            return carry
+
+        lax.fori_loop(1, chips, wait_stat, 0)
+        stat_share(core).start()
+        stat_share(1 - core).wait_recv()
+        total = jnp.sum(stats[0] + stats[1], axis=0)
+        scale = lax.rsqrt(total / jnp.float32(n * width) + 1e-05)
+        for i in range(groups):
+            rcol[i * 128:(i + 1) * 128] = spread(scale[i:i + 1], 128)
+        for copy in loads:
+            copy.wait()
+
+    def tables(stage):
         first = stage * rows
-        col = seg_col[first:first + rows]
-        same = jnp.concatenate([col] * (window // 128), axis=1) == padded[:, first:first + window]
+        lane = lax.broadcasted_iota(jnp.int32, (rows, HD), 1)
+        freq = jnp.exp(
+            -(2.0 * (lane % half).astype(f32) / HD) * jnp.log(jnp.float32(500000.0))
+        )
+        col = seg_col[pl.ds(pl.multiple_of(first, rows), rows)]
+        row = seg_row[0:1, pl.ds(pl.multiple_of(first, 128), window)]
+        same = jnp.concatenate([col] * (window // 128), axis=1) == row
         key_at = lax.broadcasted_iota(jnp.int32, (rows, window), 1) + (first - 128)
         query_at = lax.broadcasted_iota(jnp.int32, (rows, window), 0) + first
         bias[stage] = jnp.where(same & (key_at <= query_at), 0.0, -jnp.inf)
@@ -244,23 +289,6 @@
         cos_tab[stage] = jnp.cos(angle)
         sine = jnp.sin(angle)
         sin_tab[stage] = jnp.where(lane < half, -sine, sine)
-    acc_q[...] = jnp.zeros_like(acc_q)
-    acc_k[...] = jnp.zeros_like(acc_k)
-    acc_v[...] = jnp.zeros_like(acc_v)
-    acc_o[...] = jnp.zeros_like(acc_o)
-    kbuf[0:128] = jnp.zeros((128, HD), bf16)
-    vbuf[0:128] = jnp.zeros((128, HD), bf16)
-
-    def wait_stat(i, carry):
-        stat_copy(i, (me - i + n) % n).wait_recv()
-        return carry
-
-    lax.fori_loop(1, n, wait_stat, 0)
-    total = jnp.sum(stats[...], axis=0)[0:1]
-    scale = lax.rsqrt(total / jnp.float32(n * width) + 1e-05)
-    rcol[...] = spread(scale, 128)
-    for copy in loads:
-        copy.wait()
 
     def turn(values, stage):
         other = jnp.concatenate([values[:, half:], values[:, :half]], axis=1)
@@ -269,13 +297,14 @@
     def project(stage, owner):
         scale_rows = rcol[pl.ds(pl.multiple_of(stage * rows, rows), rows)]
         wide = jnp.concatenate([scale_rows] * (width // 128), axis=1)
-        block = (
-            buf[stage, owner].astype(f32) * wide * stats[owner, 4:5]
-        ).astype(bf16)
+        tile = stats[owner % 2, owner // 2]
+        gains = jnp.concatenate(
+            [tile[groups + i:groups + i + 1] for i in range(width // 128)], axis=1
+        )
+        block = (buf[stage, owner].astype(f32) * wide * gains).astype(bf16)
         depth = pl.ds(pl.multiple_of(owner * width, width), width)
         acc_q[stage] += dot(block, vq[depth])
-        acc_k[stage] += dot(block, vk[depth])
-        acc_v[stage] += dot(block, vv[depth])
+        acc_kv[stage] += dot_t(block, vkv[:, depth])
 
     def combine(stage, owner):
         depth = pl.ds(pl.multiple_of(owner * width, width), width)
@@ -290,7 +319,7 @@
         def _():
             combine(stage, owner)
 
-    def attend(stage):
+    def keys_of(stage):
         kv_copy(stage, 1 - core).wait_recv()
         low, high = kv[stage, 0], kv[stage, 1]
         keys = jnp.concatenate([low[:, :half], high[:, :half]], axis=1)
@@ -298,18 +327,17 @@
         here = pl.ds(pl.multiple_of(stage * rows + 128, 128), rows)
         kbuf[here] = turn(keys.astype(f32), stage)
         vbuf[here] = values
+
+    def attend(stage, head):
         near = pl.ds(pl.multiple_of(stage * rows, 128), window)
         key_win = kbuf[near]
         value_win = vbuf[near]
-        for head in range(heads):
-            cols = slice(head * HD, head * HD + HD)
-            query = turn(acc_q[stage, :, cols], stage)
-            scores = lax.dot_general(
-                query, key_win, (((1,), (1,)), ((), ())), preferred_element_type=f32
-            ) / jnp.sqrt(jnp.float32(HD)) + bias[stage]
-            probs = jnp.exp(scores - jnp.max(scores, axis=1, keepdims=True))
-            mass = jnp.sum(probs, axis=1, keepdims=True)
-            buf[stage + 2, me, :, cols] = (dot(probs.astype(bf16), value_win) / mass).astype(bf16)
+        cols = pl.ds(pl.multiple_of(head * HD, HD), HD)
+        query = turn(acc_q[stage, :, cols], stage)
+        scores = dot_t(query, key_win) / jnp.sqrt(jnp.float32(HD)) + bias[stage]
+        probs = jnp.exp(scores - jnp.max(scores, axis=1, keepdims=True))
+        mass = jnp.sum(probs, axis=1, keepdims=True)
+        buf[stage + 2, me, :, cols] = (dot(probs.astype(bf16), value_win) / mass).astype(bf16)
 
     def step_body(t, carry):
         stage = t // 4
@@ -319,28 +347,38 @@
         def _():
             send_own(stage + 1)
 
-        for part in range(2):
-            for way in range(2):
-                @pl.when((step < 3) | (part == way))
-                def _():
+        @pl.when(step < 3)
+        def _():
+            for part in range(PARTS):
+                for way in range(2):
                     arrival(way, stage, step, part).wait_recv()
 
-                @pl.when((step < 2) | ((step == 2) & (part == way)))
-                def _():
-                    ring(way, stage, step + 1, part).start()
-
-        @pl.when(step < 3)
-        def _():
+                    @pl.when((step < 2) | (part % 2 == way))
+                    def _():
+                        ring(way, stage, step + 1, part).start()
+
             share(stage, step + 1, pos - step - 1, True).start()
             share(stage, step + 4, pos + step + 1, True).start()
 
-        @pl.when(step == 3)
-        def _():
-            share(stage, 7, pos + 4, True).start()
+        @pl.when(t == 0)
+        def _():
+            prepare()
+
+        @pl.when((t == 1) | (t == 2))
+        def _():
+            tables(t - 1)
 
         @pl.when((step == 0) & ((stage == 1) | (stage == 2)))
         def _():
-            attend(stage - 1)
+            keys_of(stage - 1)
+
+        @pl.when((step < 2) & ((stage == 1) | (stage == 2)))
+        def _():
+            def one_head(head, carry):
+                attend(stage - 1, head)
+                return carry
+
+            lax.fori_loop(step * (heads // 2), (step + 1) * (heads // 2), one_head, 0)
 
         def unit(u, carry):
             last = u // 2
@@ -351,6 +389,13 @@
 
             @pl.when((u == 0) | ((u == 1) & (step > 0)) | ((u == 2) & (step == 3)))
             def _():
+                @pl.when(u == 2)
+                def _():
+                    for part in range(PARTS):
+                        arrival(part % 2, stage, 3, part).wait_recv()
+
+                    share(stage, 7, pos + 4, True).start()
+
                 share(stage, slot, place, False).wait_recv()
                 first = chip_at(place) * 2
 
@@ -366,9 +411,7 @@
 
         @pl.when((step == 3) & (stage < 2))
         def _():
-            kv[stage, core] = jnp.concatenate(
-                [acc_k[stage].astype(bf16), acc_v[stage].astype(bf16)], axis=1
-            )
+            kv[stage, core] = acc_kv[stage].astype(bf16)
             kv_copy(stage, core).start()
 
         return carry
@@ -383,8 +426,8 @@
     def finish(stage, carry):
         for way in range(2):
             for step in range(4):
-                for part in range(2):
-                    if step < 3 or part == way:
+                for part in range(PARTS):
+                    if step < 3 or part % 2 == way:
                         ring(way, stage, step, part).wait_send()
         for slot, away in enumerate((0, -1, -2, -3, 1, 2, 3, 4)):
             share(stage, slot, pos + away, True).wait_send()
@@ -395,10 +438,11 @@
         kv_copy(stage, core).wait_send()
 
     def left(i, carry):
-        stat_copy(i, me).wait_send()
+        stat_copy(i, chip).wait_send()
         return carry
 
-    lax.fori_loop(1, n, left, 0)
+    lax.fori_loop(1, chips, left, 0)
+    stat_share(core).wait_send()
 
 
 def ring_body(hidden_in, norm_gain, w_query, w_key, w_value, w_out, segment_ids):
@@ -419,14 +463,14 @@
         scratch_shapes=[
             pltpu.VMEM((4, n, rows, width), bf16),
             pltpu.VMEM(w_query.shape, bf16),
-            pltpu.VMEM(w_key.shape, bf16),
-            pltpu.VMEM(w_value.shape, bf16),
+            pltpu.VMEM((2 * kvw, depth), bf16),
             pltpu.VMEM(w_out.shape, bf16),
             pltpu.VMEM((2, rows, w_query.shape[1]), f32),
-            pltpu.VMEM((2, rows, kvw), f32),
-            pltpu.VMEM((2, rows, kvw), f32),
+            pltpu.VMEM((2, rows, 2 * kvw), f32),
             pltpu.VMEM((2, rows, width), f32),
-            pltpu.VMEM((n, 8, tokens), f32),
+            pltpu.VMEM((2, n // 2, (tokens + width) // 128, 128), f32),
+            pltpu.VMEM((tokens, 128), f32),
+            pltpu.VMEM((8, tokens + 128), f32),
             pltpu.VMEM((tokens, 128), f32),
             pltpu.VMEM((2, rows, HD), f32),
             pltpu.VMEM((2, rows, HD), f32),
@@ -435,12 +479,12 @@
             pltpu.VMEM((tokens + 128, HD), bf16),
             pltpu.VMEM((tokens + 128, HD), bf16),
             dma((6,)),
-            dma((2, 4, 4, 2)),
-            dma((2, 4, 4, 2)),
+            dma((2, 4, 4, PARTS)),
+            dma((2, 4, 4, PARTS)),
             dma((4, 8)),
             dma((4, 8)),
-            dma((n,)),
-            dma((n,)),
+            dma((n // 2,)),
+            dma((n // 2,)),
             dma((2,)),
             dma((2,)),
         ],
@@ -448,7 +492,7 @@
             collective_id=0, has_side_effects=True, vmem_limit_bytes=56 * 1024 * 1024
         ),
     )(
-        hidden_in, norm_gain[None, :], w_query, w_key, w_value, w_out, segment_ids[None, :]
+        hidden_in, norm_gain, w_query, w_key.T, w_value.T, w_out, segment_ids[None, :]
     )
 
 

time: 117 us -> 99.7 us (0.85)
  Pallas kernels: 108 us -> 97.6 us
  local copies, waits for them, and re-layouts: 8.63 us -> 1.87 us
    pallas_call x1, Pallas kernels: 108 us -> 97.6 us  [ring_body(): pl.pallas_call(functools.partial(fused, n), out_shape=jax.ShapeDtypeStruc...]
    unnamed x3 -> x1, local copies, waits for them, and re-layouts: 7.37 us -> 1.87 us
    broadcast_in_dim x1 -> x0, local copies, waits for them, and re-layouts: 1.26 us -> none  [ring_body(): norm_gain[None, :]]
where the time goes in v2:
time: 99.7 us; the launch traced here: 99.5 us
  Pallas kernels  97.6 us (98%)
  local copies, waits for them, and re-layouts  1.87 us (2%)
    pallas_call x1, Pallas kernels, ring_body(): pl.pallas_call(functools.partial(fused, n), out_shape=jax.ShapeDtypeStruc...  97.6 us

profile of v2, /device:TPU:1, one launch (start us, length us, event | category | flops | bytes accessed | tf_op | source)
XLA Modules:
  0.0 99.5 jit_solution(11352041876849413340)
XLA Ops:
  0.0 97.6 %shard_map.73 = bf16[512,512]{1,0:T(8,128)(2,1)} custom-call(bf16[512,512]{1,0:T(8,128)(2,1)} %hidden.1, bf16[512]{0:T(512)(128)(2,1)} %gain.1, bf16[8192,512]{1,0:T(8,128)(2,1)} %w_query.1, bf16[64,8192]{1,0:T(8,128)(2,1)} %bitcast.3, bf16[64,8192]{1,0:T(8,128)(2,1)} %bitcast.4, bf16[8192,512]{1,0:T(8,128)(2,1)} %w_out.1, s32[1,512]{1,0:T(1,128)} %bitcast.5), custom_call_target="tpu_custom_call" | custom-call | tf_op jit(solution)/shard_map/pallas_call | solution.py:458
  97.6 1.9 %copy.9 = bf16[512,512]{1,0:T(8,128)(2,1)} copy(bf16[512,512]{1,0:T(8,128)(2,1)} %shard_map.73) | data formatting | bytes 1048576

commit v3 on v2

--- a/solution.py
+++ b/solution.py
@@ -169,11 +169,19 @@
         ref = buf.at[stage, owner]
         return remote(ref, ref, sib_send.at[stage, slot], sib_recv.at[stage, slot], sib)
 
-    def send_own(stage):
-        for part in range(PARTS):
+    def send_parts(stage, parts):
+        for part in parts:
             for way in range(2):
                 ring(way, stage, 0, part).start()
+
+    def send_own(stage):
+        send_parts(stage, range(PARTS))
         share(stage, 0, pos, True).start()
+
+    def share_part(stage, part, own):
+        owner = chip_at(pos + 4) * 2 + (core if own else 1 - core)
+        ref = buf.at[stage, owner, pl.ds(part * piece, piece)]
+        return remote(ref, ref, sib_send.at[stage, 7 + part], sib_recv.at[stage, 7 + part], sib)
 
     def kv_copy(stage, side):
         ref = kv.at[stage, side]
@@ -198,9 +206,6 @@
             )
         )
     ]
-    for copy in loads:
-        copy.start()
-
     barrier = pltpu.get_barrier_semaphore()
 
     def greet(i, carry):
@@ -226,6 +231,10 @@
     seg_col[...] = spread(ids, 128)
     for copy in own_x:
         copy.wait()
+    for copy in loads:
+        copy.start()
+    pl.semaphore_wait(barrier, chips)
+    send_parts(0, range(PARTS // 2))
 
     groups = tokens // 128
     lines = []
@@ -250,9 +259,9 @@
         stat_copy(i, chip).start()
         return carry
 
-    pl.semaphore_wait(barrier, chips)
     lax.fori_loop(1, chips, send_stat, 0)
-    send_own(0)
+    send_parts(0, range(PARTS // 2, PARTS))
+    share(0, 0, pos, True).start()
 
     def prepare():
         def wait_stat(i, carry):
@@ -266,7 +275,7 @@
         scale = lax.rsqrt(total / jnp.float32(n * width) + 1e-05)
         for i in range(groups):
             rcol[i * 128:(i + 1) * 128] = spread(scale[i:i + 1], 128)
-        for copy in loads:
+        for copy in loads[:3]:
             copy.wait()
 
     def tables(stage):
@@ -347,67 +356,74 @@
         def _():
             send_own(stage + 1)
 
-        @pl.when(step < 3)
+        def one_part(part, carry):
+            for way in range(2):
+                @pl.when((step < 3) | (part % 2 == way))
+                def _():
+                    arrival(way, stage, step, part).wait_recv()
+
+                @pl.when((step < 2) | ((step == 2) & (part % 2 == way)))
+                def _():
+                    ring(way, stage, step + 1, part).start()
+
+            @pl.when(step == 3)
+            def _():
+                share_part(stage, part, True).start()
+
+            @pl.when((step < 3) & (part == PARTS - 1))
+            def _():
+                share(stage, step + 1, pos - step - 1, True).start()
+                share(stage, step + 4, pos + step + 1, True).start()
+
+            @pl.when((t == 0) & (part == 2))
+            def _():
+                prepare()
+
+            @pl.when(((t == 1) | (t == 2)) & (part == 1))
+            def _():
+                tables(t - 1)
+
+            @pl.when((t == 7) & (part == 0))
+            def _():
+                loads[3].wait()
+
+            head = part + 2 * step
+            behind = (stage == 1) | (stage == 2)
+
+            @pl.when(behind & (step == 0) & (part == 0))
+            def _():
+                keys_of(stage - 1)
+
+            @pl.when(behind & (part < 2) & (head < heads))
+            def _():
+                attend(stage - 1, head)
+
+            left = part // 2
+            place = pos - step * (1 - left) + step * left
+            slot = step * (1 - left) + (step + 3) * left * ((step + 2) // 3)
+
+            @pl.when((step > 0) | (left == 1))
+            def _():
+                @pl.when(part % 2 == 0)
+                def _():
+                    share(stage, slot, place, False).wait_recv()
+
+                use(stage, chip_at(place) * 2 + part % 2)
+
+            return carry
+
+        lax.fori_loop(0, PARTS, one_part, 0)
+
+        @pl.when(step == 3)
         def _():
             for part in range(PARTS):
-                for way in range(2):
-                    arrival(way, stage, step, part).wait_recv()
-
-                    @pl.when((step < 2) | (part % 2 == way))
-                    def _():
-                        ring(way, stage, step + 1, part).start()
-
-            share(stage, step + 1, pos - step - 1, True).start()
-            share(stage, step + 4, pos + step + 1, True).start()
-
-        @pl.when(t == 0)
-        def _():
-            prepare()
-
-        @pl.when((t == 1) | (t == 2))
-        def _():
-            tables(t - 1)
-
-        @pl.when((step == 0) & ((stage == 1) | (stage == 2)))
-        def _():
-            keys_of(stage - 1)
-
-        @pl.when((step < 2) & ((stage == 1) | (stage == 2)))
-        def _():
-            def one_head(head, carry):
-                attend(stage - 1, head)
+                share_part(stage, part, False).wait_recv()
+
+            def far(k, carry):
+                use(stage, chip_at(pos + 4) * 2 + k)
                 return carry
 
-            lax.fori_loop(step * (heads // 2), (step + 1) * (heads // 2), one_head, 0)
-
-        def unit(u, carry):
-            last = u // 2
-            left = u % 2
-            right = 1 - left - last
-            place = pos - step * right + step * left + 4 * last
-            slot = step * right + (step + 3) * left + 7 * last
-
-            @pl.when((u == 0) | ((u == 1) & (step > 0)) | ((u == 2) & (step == 3)))
-            def _():
-                @pl.when(u == 2)
-                def _():
-                    for part in range(PARTS):
-                        arrival(part % 2, stage, 3, part).wait_recv()
-
-                    share(stage, 7, pos + 4, True).start()
-
-                share(stage, slot, place, False).wait_recv()
-                first = chip_at(place) * 2
-
-                def one(k, carry):
-                    use(stage, first + k)
-                    return carry
-
-                lax.fori_loop(0, 2, one, 0)
-
-            return carry
-
-        lax.fori_loop(0, 3, unit, 0)
+            lax.fori_loop(0, 2, far, 0)
 
         @pl.when((step == 3) & (stage < 2))
         def _():
@@ -429,8 +445,10 @@
                 for part in range(PARTS):
                     if step < 3 or part % 2 == way:
                         ring(way, stage, step, part).wait_send()
-        for slot, away in enumerate((0, -1, -2, -3, 1, 2, 3, 4)):
+        for slot, away in enumerate((0, -1, -2, -3, 1, 2, 3)):
             share(stage, slot, pos + away, True).wait_send()
+        for part in range(PARTS):
+            share_part(stage, part, True).wait_send()
         return carry
 
     lax.fori_loop(0, 4, finish, 0)
@@ -481,8 +499,8 @@
             dma((6,)),
             dma((2, 4, 4, PARTS)),
             dma((2, 4, 4, PARTS)),
-            dma((4, 8)),
-            dma((4, 8)),
+            dma((4, 7 + PARTS)),
+            dma((4, 7 + PARTS)),
             dma((n // 2,)),
             dma((n // 2,)),
             dma((2,)),

time: 99.7 us -> 97 us (0.973)
  Pallas kernels: 97.6 us -> 94.9 us
    pallas_call x1, Pallas kernels: 97.6 us -> 94.9 us  [ring_body(): pl.pallas_call(functools.partial(fused, n), out_shape=jax.ShapeDtypeStruc...]
where the time goes in v3:
time: 97 us; the launch traced here: 96.8 us
  Pallas kernels  94.9 us (98%)
  local copies, waits for them, and re-layouts  1.87 us (2%)
    pallas_call x1, Pallas kernels, ring_body(): pl.pallas_call(functools.partial(fused, n), out_shape=jax.ShapeDtypeStruc...  94.9 us

profile of v3, /device:TPU:1, one launch (start us, length us, event | category | flops | bytes accessed | tf_op | source)
XLA Modules:
  0.0 96.8 jit_solution(16912458749695387204)
XLA Ops:
  0.0 94.9 %shard_map.73 = bf16[512,512]{1,0:T(8,128)(2,1)} custom-call(bf16[512,512]{1,0:T(8,128)(2,1)} %hidden.1, bf16[512]{0:T(512)(128)(2,1)} %gain.1, bf16[8192,512]{1,0:T(8,128)(2,1)} %w_query.1, bf16[64,8192]{1,0:T(8,128)(2,1)} %bitcast.3, bf16[64,8192]{1,0:T(8,128)(2,1)} %bitcast.4, bf16[8192,512]{1,0:T(8,128)(2,1)} %w_out.1, s32[1,512]{1,0:T(1,128)} %bitcast.5), custom_call_target="tpu_custom_call" | custom-call | tf_op jit(solution)/shard_map/pallas_call | solution.py:476
  94.9 1.9 %copy.9 = bf16[512,512]{1,0:T(8,128)(2,1)} copy(bf16[512,512]{1,0:T(8,128)(2,1)} %shard_map.73) | data formatting | bytes 1048576

commit v4 on v3

--- a/solution.py
+++ b/solution.py
@@ -113,7 +113,7 @@
     n, hidden, gain, w_query, w_key, w_value, w_out, seg, out,
     buf, vq, vkv, vo, acc_q, acc_kv, acc_o, stats, rcol, seg_row, seg_col, cos_tab, sin_tab, bias,
     kv, kbuf, vbuf, load_sem, ring_send, ring_recv, sib_send, sib_recv,
-    stat_send, stat_recv, kv_send, kv_recv,
+    stat_send, stat_recv, kv_send, kv_recv, mixed, out_sem,
 ):
     f32, bf16 = jnp.float32, jnp.bfloat16
     tokens, width = hidden.shape
@@ -231,10 +231,10 @@
     seg_col[...] = spread(ids, 128)
     for copy in own_x:
         copy.wait()
+    pl.semaphore_wait(barrier, chips)
+    send_parts(0, range(PARTS // 2))
     for copy in loads:
         copy.start()
-    pl.semaphore_wait(barrier, chips)
-    send_parts(0, range(PARTS // 2))
 
     groups = tokens // 128
     lines = []
@@ -348,6 +348,10 @@
         mass = jnp.sum(probs, axis=1, keepdims=True)
         buf[stage + 2, me, :, cols] = (dot(probs.astype(bf16), value_win) / mass).astype(bf16)
 
+    def result(stage):
+        here = pl.ds(stage * rows, rows)
+        return pltpu.make_async_copy(mixed.at[here], out.at[here], out_sem.at[stage])
+
     def step_body(t, carry):
         stage = t // 4
         step = t % 4
@@ -425,6 +429,17 @@
 
             lax.fori_loop(0, 2, far, 0)
 
+            @pl.when(stage >= 2)
+            def _():
+                own = stage - 2
+                mixed[pl.ds(pl.multiple_of(own * rows, rows), rows)] = (
+                    buf[own, me].astype(f32) + acc_o[own]
+                ).astype(bf16)
+
+            @pl.when(stage == 2)
+            def _():
+                result(0).start()
+
         @pl.when((step == 3) & (stage < 2))
         def _():
             kv[stage, core] = acc_kv[stage].astype(bf16)
@@ -434,10 +449,9 @@
 
     lax.fori_loop(0, 16, step_body, 0)
 
-    for stage in range(2):
-        out[stage * rows:(stage + 1) * rows] = (
-            buf[stage, me].astype(f32) + acc_o[stage]
-        ).astype(bf16)
+    result(1).start()
+    result(0).wait()
+    result(1).wait()
 
     def finish(stage, carry):
         for way in range(2):
@@ -477,7 +491,7 @@
         functools.partial(fused, n),
         out_shape=jax.ShapeDtypeStruct((tokens, width), bf16),
         in_specs=[anywhere, vmem, anywhere, anywhere, anywhere, anywhere, vmem],
-        out_specs=vmem,
+        out_specs=anywhere,
         scratch_shapes=[
             pltpu.VMEM((4, n, rows, width), bf16),
             pltpu.VMEM(w_query.shape, bf16),
@@ -505,6 +519,8 @@
             dma((n // 2,)),
             dma((2,)),
             dma((2,)),
+            pltpu.VMEM((tokens, width), bf16),
+            dma((2,)),
         ],
         compiler_params=pltpu.CompilerParams(
             collective_id=0, has_side_effects=True, vmem_limit_bytes=56 * 1024 * 1024

time: 97 us -> 97 us (level)
  no operation moved by 1% of the time
where the time goes in v4:
time: 97 us; the launch traced here: 96.8 us
  Pallas kernels  94.9 us (98%)
  local copies, waits for them, and re-layouts  1.87 us (2%)
    pallas_call x1, Pallas kernels, ring_body(): pl.pallas_call(functools.partial(fused, n), out_shape=jax.ShapeDtypeStruc...  94.9 us

profile of v4, /device:TPU:1, one launch (start us, length us, event | category | flops | bytes accessed | tf_op | source)
XLA Modules:
  0.0 96.8 jit_solution(11505649971344753205)
XLA Ops:
  0.0 94.9 %shard_map.73 = bf16[512,512]{1,0:T(8,128)(2,1)} custom-call(bf16[512,512]{1,0:T(8,128)(2,1)} %hidden.1, bf16[512]{0:T(512)(128)(2,1)} %gain.1, bf16[8192,512]{1,0:T(8,128)(2,1)} %w_query.1, bf16[64,8192]{1,0:T(8,128)(2,1)} %bitcast.3, bf16[64,8192]{1,0:T(8,128)(2,1)} %bitcast.4, bf16[8192,512]{1,0:T(8,128)(2,1)} %w_out.1, s32[1,512]{1,0:T(1,128)} %bitcast.5), custom_call_target="tpu_custom_call" | custom-call | tf_op jit(solution)/shard_map/pallas_call | solution.py:490
  94.9 1.9 %copy.9 = bf16[512,512]{1,0:T(8,128)(2,1)} copy(bf16[512,512]{1,0:T(8,128)(2,1)} %shard_map.73) | data formatting | bytes 1048576
